TPU v7x, 256 devices: a whole 4x4x8 slice. The times are simulated.
256 devices in a mesh: gx: 8 (over x, core), gy: 32 (over z, y).
Axes of the slice: x: 4, y: 4, z: 8, core: 2. Of those that a mesh axis runs over, the one named last changes fastest.
Arguments:
- state_field: float32 [256, 512, 16, 256], P('gx', 'gy'), may hold values from -80 to 80
- start_basis: float32 [256, 32], replicated, may hold values from -6 to 6
Outputs:
- core_tensor: float32 [256, 512, 512], P('gx', 'gy')
- z_factor: float32 [256, 32], replicated
- x_triangle: float32 [256, 256], replicated
All inputs are finite; a program needn't handle non-finite values.
Results may differ from a plain program's by a relative error of at most 0.0003.
Values sent between devices are 32-bit elements; how exact they have to be, the bound alone decides.
A program may use at most 64 MiB of HBM per device.

v0:
```python
import jax
import jax.numpy as jnp
from jax import lax
from jax.sharding import PartitionSpec as P

ITERS = 3
precise = lax.Precision.HIGHEST


def orthonormal(image):
    for repeat in range(2):
        inner_gram = jnp.dot(image.T, image, precision=precise, preferred_element_type=jnp.float32)
        lower_factor = jnp.linalg.cholesky(inner_gram)
        image = lax.linalg.triangular_solve(
            lower_factor, image, left_side=False, lower=True, transpose_a=True
        )
    return image


def local(state_field, start_basis):
    x_cells, y_cells, species, z_cells = state_field.shape
    unfolded = state_field.reshape(x_cells * y_cells * species, z_cells)
    local_gram = lax.dot_general(
        unfolded,
        unfolded,
        (((0,), (0,)), ((), ())),
        precision=precise,
        preferred_element_type=jnp.float32,
    )
    z_basis = start_basis
    gram_z = lax.psum(local_gram, ("gx", "gy"))
    for iteration in range(ITERS):
        z_basis = orthonormal(
            jnp.dot(gram_z, z_basis, precision=precise, preferred_element_type=jnp.float32)
        )
    rank_kept = z_basis.shape[1]
    core_rows = jnp.dot(unfolded, z_basis, precision=precise, preferred_element_type=jnp.float32)
    core_tensor = core_rows.reshape(x_cells, y_cells, species * rank_kept)
    x_total = x_cells * lax.axis_size("gx")
    regrouped = lax.all_to_all(core_tensor, "gx", split_axis=2, concat_axis=0, tiled=True)
    x_rows = regrouped.reshape(x_total, -1)
    local_xgram = jnp.dot(x_rows, x_rows.T, precision=precise, preferred_element_type=jnp.float32)
    gram_x = lax.psum(local_xgram, ("gx", "gy"))
    column_count = y_cells * lax.axis_size("gy") * species * rank_kept
    x_triangle = jnp.linalg.cholesky(gram_x).T / jnp.sqrt(jnp.float32(column_count))
    return (core_tensor, z_basis, x_triangle)


def solution(mesh):
    return jax.shard_map(
        local,
        mesh=mesh,
        in_specs=(P("gx", "gy", None, None), P()),
        out_specs=(P("gx", "gy", None), P(), P()),
        check_vma=False,
    )
```

profile of v0, /device:TPU:2, one launch (start us, length us, event | category | flops | bytes accessed | tf_op | source)
XLA Modules:
  0.0 675.3 jit_solution(2987790697292606197)
XLA Ops:
  7.2 17.8 %convolution_bitcast_fusion.1 = f32[256,256]{1,0:T(8,128)} fusion(f32[32,16,16,256]{3,2,1,0:T(8,128)} %param.5), kind=kOutput, calls=%fused_computation.1 | convolution fusion | flops 6442450944 | bytes 8650752 | tf_op jit(solution)/shard_map/dot_general | solution.py:23
  25.3 253.2 %all-reduce.4.cloned.1.call-done = f32[256,256]{1,0:T(8,128)} async-done(((f32[256,256]{1,0:T(8,128)}), f32[256,256]{1,0:T(8,128)}) %all-reduce.4.cloned.1.call-update) | async-done | bytes 262160 | tf_op jit(solution)/shard_map/psum | solution.py:31
  278.4 1.3 fusion.32
  280.0 2.9 cholesky.222
  282.9 0.6 compare_reduce_fusion.5
  283.6 0.7 fusion.4
  284.2 2.4 custom-call.22
  287.2 2.9 cholesky.233
  290.1 0.6 compare_reduce_fusion.4
  290.8 0.7 fusion.5
  291.4 2.4 custom-call.23
  294.1 1.3 fusion.35
  295.7 2.9 cholesky.244
  298.6 0.6 compare_reduce_fusion.3
  299.3 0.7 fusion.6
  299.9 2.4 custom-call.24
  302.9 2.9 cholesky.255
  305.8 0.6 compare_reduce_fusion.2
  306.5 0.7 fusion.7
  307.1 2.4 custom-call.25
  309.8 1.3 fusion.38
  311.3 2.9 cholesky.266
  314.3 0.6 compare_reduce_fusion.1
  314.9 0.7 fusion.8
  315.6 2.4 custom-call.26
  318.5 2.9 cholesky.277
  321.5 0.6 compare_reduce_fusion
  322.1 0.7 fusion.9
  322.8 2.4 custom-call.27
  325.5 9.9 %convolution_bitcast_fusion = f32[8192,32]{0,1:T(8,128)S(1)} fusion(f32[256,32]{0,1:T(8,128)S(1)} %convolution_bitcast_fusion.2, f32[8192,256]{1,0:T(8,128)} %bitcast.127), kind=kOutput, calls=%fused_computation | convolution fusion | flops 805306368 | bytes 9469952 | tf_op jit(solution)/shard_map/dot_general | solution.py:37
  335.4 2.6 copy.47
  338.0 3.5 reshape.41
  341.6 3.8 copy.48
  345.4 3.9 reshape.66
  349.3 19.2 %all_to_all.15 = f32[8,1,32768]{2,1,0:T(1,128)S(1)} all-to-all(f32[8,1,32768]{2,1,0:T(1,128)S(1)} %reshape.66), channel_id=1, replica_groups=mesh['gx'=8,'gy'=32] {'gx'}, dimensions={0} | all-to-all | bytes 2097152 | tf_op jit(solution)/shard_map/all_to_all | solution.py:40
  369.1 3.1 reduce.16
  372.2 3.3 reshape.67
  375.5 3.6 copy.49
  379.2 0.6 reshape.42
  379.7 1.7 fusion.41
  381.5 248.1 %all-reduce.6.cloned.1.call-done = f32[256,256]{0,1:T(8,128)} async-done(((f32[256,256]{0,1:T(8,128)}), f32[256,256]{0,1:T(8,128)}) %all-reduce.6.cloned.1.call-update) | async-done | bytes 262160 | tf_op jit(solution)/shard_map/psum | solution.py:43
  629.6 1.1 copy.51
  630.7 1.0 fusion
  631.7 11.7 %cholesky.77 = f32[128,128]{1,0:T(8,128)S(1)} custom-call(f32[128,128]{1,0:T(8,128)S(1)} %cholesky.286), custom_call_target="Cholesky" | custom-call | tf_op jit(solution)/shard_map/jit(cholesky)/cholesky | solution.py:45
  643.4 9.8 %custom-call.16 = f32[1,128,128]{1,2,0:T(8,128)S(1)} custom-call(f32[1,128,128]{2,1,0:T(8,128)S(1)} %get-tuple-element.20), custom_call_target="InvertDiagBlocksLowerTriangular" | custom-call | tf_op jit(solution)/shard_map/jit(cholesky)/cholesky | solution.py:45
  653.8 11.7 %cholesky.132 = f32[128,128]{1,0:T(8,128)S(1)} custom-call(f32[128,128]{1,0:T(8,128)S(1)} %convolution_subtract_fusion), custom_call_target="Cholesky" | custom-call | tf_op jit(solution)/shard_map/jit(cholesky)/cholesky | solution.py:45
  665.5 0.7 compare_reduce_fusion.6
  667.6 0.8 copy.52
  (48 shorter events, 4.5 us)
Async XLA Ops:
  7.2 271.3 %copy-start = (f32[256,32]{0,1:T(8,128)S(1)}, f32[256,32]{0,1:T(8,128)}, u32[]{:S(2)}) copy-start(f32[256,32]{0,1:T(8,128)} %param.6) | copy-start | bytes 98308
  7.2 271.2 %all-reduce.4.cloned.1.call-start = ((), (), s32[]{:S(2)}) async-start(), calls=%async_computation.1 | async-start | bytes 524288 | tf_op jit(solution)/shard_map/psum | solution.py:31
  25.0 604.6 %all-reduce.6.cloned.1.call-start = ((), (), s32[]{:S(2)}) async-start(), calls=%async_computation.2 | async-start | bytes 524288 | tf_op jit(solution)/shard_map/psum | solution.py:43
  325.5 16.1 %copy-start.2 = (f32[256,32]{0,1:T(8,128)}, f32[256,32]{0,1:T(8,128)S(1)}, u32[]{:S(2)}) copy-start(f32[256,32]{0,1:T(8,128)S(1)} %convolution_bitcast_fusion.2) | copy-start | bytes 98308
  341.6 34.0 %copy-start.1 = (f32[32,16,512]{2,1,0:T(8,128)}, f32[32,16,512]{2,1,0:T(8,128)S(1)}, u32[]{:S(2)}) copy-start(f32[32,16,512]{2,1,0:T(8,128)S(1)} %reshape.41) | copy-start | bytes 3145732
Sparse Core Ops, SparseCore 0:
  25.2 253.2 all-reduce.3
  381.6 247.9 all-reduce.5
where the time goes:
time: 676 us; the launch traced here: 675 us
  waiting for transfers between devices  501 us (74%)
  other arithmetic  78.3 us (12%)
  matrix products  36.2 us (5%)
  local copies, waits for them, and re-layouts  24.3 us (4%)
  blocking collectives  19.2 us (3%)
  between operations  15.7 us (2%)
    psum x1, waiting for transfers between devices, local(): gram_z = lax.psum(local_gram, ('gx', 'gy'))  253 us
    psum x1, waiting for transfers between devices, local(): gram_x = lax.psum(local_xgram, ('gx', 'gy'))  248 us
    another operation x6, other arithmetic, local(): jnp.linalg.cholesky(gram_x).T / jnp.sqrt(jnp.float32(column_count))  34 us
    another operation x18, other arithmetic, orthonormal(): lower_factor = jnp.linalg.cholesky(inner_gram)  21.6 us
    all_to_all x1, blocking collectives, local(): lax.all_to_all(core_tensor, 'gx', split_axis=2, concat_axis=0, tiled=True)  19.2 us
    another operation x12, other arithmetic, orthonormal(): lax.linalg.triangular_solve(lower_factor, image, left_side=False, lower=T...  18.5 us
    dot_general x1, matrix products, local(): lax.dot_general(unfolded, unfolded, (((0,), (0,)), ((), ())), precision=p...  17.8 us
  transfers between devices with their start and end apart: 2, of which 2 were waited for; matrix products, arithmetic and copies ran while one was open for 0% of the time, Pallas kernels for 0%

commit v1 on v0

--- a/solution.py
+++ b/solution.py
@@ -37,7 +37,19 @@
     core_rows = jnp.dot(unfolded, z_basis, precision=precise, preferred_element_type=jnp.float32)
     core_tensor = core_rows.reshape(x_cells, y_cells, species * rank_kept)
     x_total = x_cells * lax.axis_size("gx")
-    regrouped = lax.all_to_all(core_tensor, "gx", split_axis=2, concat_axis=0, tiled=True)
+    ways, here = (lax.axis_size("gx"), lax.axis_index("gx"))
+    width = core_tensor.shape[2] // ways
+    dims = list(core_tensor.shape)
+    dims[2] = width
+    height = dims[0]
+    dims[0] = height * ways
+    full = jnp.zeros(dims, core_tensor.dtype)
+    for mask in range(ways):
+        part = lax.dynamic_slice_in_dim(core_tensor, (here ^ mask) * width, width, axis=2)
+        if mask:
+            part = lax.ppermute(part, "gx", [(d, d ^ mask) for d in range(ways)])
+        full = lax.dynamic_update_slice_in_dim(full, part, (here ^ mask) * height, axis=0)
+    regrouped = full
     x_rows = regrouped.reshape(x_total, -1)
     local_xgram = jnp.dot(x_rows, x_rows.T, precision=precise, preferred_element_type=jnp.float32)
     gram_x = lax.psum(local_xgram, ("gx", "gy"))

time: 676 us -> 690 us (1.021)
  local copies, waits for them, and re-layouts: 24.3 us -> 43.6 us
  blocking collectives: 19.2 us -> 0 us
  starting transfers between devices: 0.26 us -> 7.58 us
    dynamic_update_slice x0 -> x8, local copies, waits for them, and re-layouts: none -> 24.9 us  [local(): lax.dynamic_update_slice_in_dim(full, part, (here ^ mask) * height, axis=0)]
    all_to_all x1 -> x0, blocking collectives: 19.2 us -> none  [local(): lax.all_to_all(core_tensor, 'gx', split_axis=2, concat_axis=0, tiled=True)]
    ppermute x0 -> x7, local copies, waits for them, and re-layouts: none -> 8.15 us  [local(): part = lax.ppermute(part, 'gx', [(d, d ^ mask) for d in range(ways)])]
    ppermute x0 -> x7, starting transfers between devices: none -> 7.04 us  [local(): part = lax.ppermute(part, 'gx', [(d, d ^ mask) for d in range(ways)])]
    unnamed x9 -> x11, local copies, waits for them, and re-layouts: 8.08 us -> 1.15 us
  transfers between devices with their start and end apart: 2 -> 9, of which waited for: 2 -> 3; matrix products, arithmetic and copies ran while one was open for 0% -> 4% of each run, Pallas kernels for 0% -> 0%
where the time goes in v1:
time: 690 us; the launch traced here: 684 us
  waiting for transfers between devices  505 us (73%)
  other arithmetic  75.2 us (11%)
  local copies, waits for them, and re-layouts  43.6 us (6%)
  matrix products  37 us (5%)
  between operations  16.1 us (2%)
  starting transfers between devices  7.58 us (1%)
    psum x1, waiting for transfers between devices, local(): gram_z = lax.psum(local_gram, ('gx', 'gy'))  253 us
    psum x1, waiting for transfers between devices, local(): gram_x = lax.psum(local_xgram, ('gx', 'gy'))  249 us
    another operation x6, other arithmetic, local(): jnp.linalg.cholesky(gram_x).T / jnp.sqrt(jnp.float32(column_count))  34 us
    dynamic_update_slice x8, local copies, waits for them, and re-layouts, local(): lax.dynamic_update_slice_in_dim(full, part, (here ^ mask) * height, axis=0)  24.9 us
    another operation x18, other arithmetic, orthonormal(): lower_factor = jnp.linalg.cholesky(inner_gram)  21.6 us
    another operation x12, other arithmetic, orthonormal(): lax.linalg.triangular_solve(lower_factor, image, left_side=False, lower=T...  18.5 us
    dot_general x1, matrix products, local(): lax.dot_general(unfolded, unfolded, (((0,), (0,)), ((), ())), precision=p...  17.8 us
  transfers between devices with their start and end apart: 9, of which 3 were waited for; matrix products, arithmetic and copies ran while one was open for 4% of the time, Pallas kernels for 0%

profile of v1, /device:TPU:2, one launch (start us, length us, event | category | flops | bytes accessed | tf_op | source)
XLA Modules:
  0.0 684.1 jit_solution(1794165583123369553)
XLA Ops:
  7.2 17.8 %convolution_bitcast_fusion.2 = f32[256,256]{1,0:T(8,128)} fusion(f32[32,16,16,256]{3,2,1,0:T(8,128)} %param.5), kind=kOutput, calls=%fused_computation.2 | convolution fusion | flops 6442450944 | bytes 8650752 | tf_op jit(solution)/shard_map/dot_general | solution.py:23
  25.6 252.8 %all-reduce.4.cloned.1.call-done = f32[256,256]{1,0:T(8,128)} async-done(((f32[256,256]{1,0:T(8,128)}), f32[256,256]{1,0:T(8,128)}) %all-reduce.4.cloned.1.call-update) | async-done | bytes 262160 | tf_op jit(solution)/shard_map/psum | solution.py:31
  278.4 1.3 fusion.32
  280.0 2.9 cholesky.222
  284.2 2.4 custom-call.22
  287.2 2.9 cholesky.233
  291.4 2.4 custom-call.23
  294.1 1.3 fusion.35
  295.7 2.9 cholesky.244
  299.9 2.4 custom-call.24
  302.9 2.9 cholesky.255
  307.1 2.4 custom-call.25
  309.8 1.3 fusion.38
  311.3 2.9 cholesky.266
  315.6 2.4 custom-call.26
  318.5 2.9 cholesky.277
  322.8 2.4 custom-call.27
  325.5 9.9 %convolution_bitcast_fusion = f32[8192,32]{0,1:T(8,128)S(1)} fusion(f32[256,32]{0,1:T(8,128)S(1)} %convolution_bitcast_fusion.3, f32[8192,256]{1,0:T(8,128)} %bitcast.120), kind=kOutput, calls=%fused_computation | convolution fusion | flops 805306368 | bytes 9469952 | tf_op jit(solution)/shard_map/dot_general | solution.py:37
  335.4 2.6 copy.32
  338.0 3.5 reshape.38
  341.6 1.4 constant_dynamic-slice_fusion
  343.4 1.5 collective-permute-start.2
  344.8 2.2 collective-permute-start.3
  347.1 1.1 collective-permute-start.4
  348.1 1.5 collective-permute-start.5
  349.6 2.5 collective-permute-done.1
  353.1 3.9 dynamic_update_slice.24
  357.0 1.2 copy.34
  358.2 3.9 dynamic_update_slice.25
  362.0 1.2 copy.35
  363.2 1.3 dynamic_update_slice.26
  364.5 1.2 copy.36
  365.7 3.9 dynamic_update_slice.27
  369.6 1.2 copy.37
  370.8 3.6 dynamic_update_slice.28
  374.4 1.2 copy.38
  375.5 3.6 dynamic_update_slice.29
  379.1 1.2 copy.39
  380.3 1.0 dynamic_update_slice.30
  381.4 1.2 copy.40
  382.5 3.8 dynamic_update_slice.31
  386.3 2.5 convolution_bitcast_fusion.1
  388.9 249.3 %all-reduce.6.cloned.1.call-done = f32[256,256]{0,1:T(8,128)} async-done(((f32[256,256]{0,1:T(8,128)}), f32[256,256]{0,1:T(8,128)}) %all-reduce.6.cloned.1.call-update) | async-done | bytes 262160 | tf_op jit(solution)/shard_map/psum | solution.py:55
  638.2 1.1 copy.42
  639.3 1.0 fusion
  640.3 11.7 %cholesky.77 = f32[128,128]{1,0:T(8,128)S(1)} custom-call(f32[128,128]{1,0:T(8,128)S(1)} %cholesky.286), custom_call_target="Cholesky" | custom-call | tf_op jit(solution)/shard_map/jit(cholesky)/cholesky | solution.py:57
  652.0 9.8 %custom-call.16 = f32[1,128,128]{1,2,0:T(8,128)S(1)} custom-call(f32[1,128,128]{2,1,0:T(8,128)S(1)} %get-tuple-element.22), custom_call_target="InvertDiagBlocksLowerTriangular" | custom-call | tf_op jit(solution)/shard_map/jit(cholesky)/cholesky | solution.py:57
  662.3 11.7 %cholesky.132 = f32[128,128]{1,0:T(8,128)S(1)} custom-call(f32[128,128]{1,0:T(8,128)S(1)} %convolution_subtract_fusion), custom_call_target="Cholesky" | custom-call | tf_op jit(solution)/shard_map/jit(cholesky)/cholesky | solution.py:57
  (76 shorter events, 15.1 us)
Async XLA Ops:
  7.2 271.3 %copy-start = (f32[256,32]{0,1:T(8,128)S(1)}, f32[256,32]{0,1:T(8,128)}, u32[]{:S(2)}) copy-start(f32[256,32]{0,1:T(8,128)} %param.6) | copy-start | bytes 98308
  7.2 271.2 %all-reduce.4.cloned.1.call-start = ((), (), s32[]{:S(2)}) async-start(), calls=%async_computation | async-start | bytes 524288 | tf_op jit(solution)/shard_map/psum | solution.py:31
  25.0 613.1 %all-reduce.6.cloned.1.call-start = ((), (), s32[]{:S(2)}) async-start(), calls=%async_computation.1 | async-start | bytes 524288 | tf_op jit(solution)/shard_map/psum | solution.py:55
  325.5 16.1 %copy-start.4 = (f32[256,32]{0,1:T(8,128)}, f32[256,32]{0,1:T(8,128)S(1)}, u32[]{:S(2)}) copy-start(f32[256,32]{0,1:T(8,128)S(1)} %convolution_bitcast_fusion.3) | copy-start | bytes 98308
  341.6 38.7 %copy-start.1 = (f32[32,16,512]{2,1,0:T(8,128)}, f32[32,16,512]{2,1,0:T(8,128)S(1)}, u32[]{:S(2)}) copy-start(f32[32,16,512]{2,1,0:T(8,128)S(1)} %reshape.38) | copy-start | bytes 3145732
  343.0 5.2 collective-permute-start
  343.0 9.1 %collective-permute-start.1 = (f32[32,16,64]{2,1,0:T(8,128)S(1)}, f32[32,16,64]{2,1,0:T(8,128)S(1)}, u32[]{:S(2)}, u32[]{:S(2)}) collective-permute-start(f32[32,16,64]{2,1,0:T(8,128)S(1)} %get-tuple-element.16), channel_id=1, source_target_pairs={{0,64},{32,96},{64,0},{96,32},{128,192},{160,224},{192,128},{224,1... | collective-permute-start | bytes 393224 | tf_op jit(solution)/shard_map/ppermute | solution.py:50
  343.4 21.2 %collective-permute-start.2 = (f32[32,16,64]{2,1,0:T(8,128)}, f32[32,16,64]{2,1,0:T(8,128)}, u32[]{:S(2)}, u32[]{:S(2)}) collective-permute-start(f32[32,16,64]{2,1,0:T(8,128)} %get-tuple-element.15), channel_id=1, source_target_pairs={{0,96},{32,64},{64,32},{96,0},{128,224},{160,192},{192,160},{224,1... | collective-permute-start | bytes 393224 | tf_op jit(solution)/shard_map/ppermute | solution.py:50
  344.8 24.7 %collective-permute-start.3 = (f32[32,16,64]{2,1,0:T(8,128)}, f32[32,16,64]{2,1,0:T(8,128)}, u32[]{:S(2)}, u32[]{:S(2)}) collective-permute-start(f32[32,16,64]{2,1,0:T(8,128)} %get-tuple-element.14), channel_id=1, source_target_pairs={{0,128},{32,160},{64,192},{96,224},{128,0},{160,32},{192,64},{224,... | collective-permute-start | bytes 393224 | tf_op jit(solution)/shard_map/ppermute | solution.py:50
  347.1 27.3 %collective-permute-start.4 = (f32[32,16,64]{2,1,0:T(8,128)S(1)}, f32[32,16,64]{2,1,0:T(8,128)}, u32[]{:S(2)}, u32[]{:S(2)}) collective-permute-start(f32[32,16,64]{2,1,0:T(8,128)S(1)} %get-tuple-element.13), channel_id=1, source_target_pairs={{0,160},{32,128},{64,224},{96,192},{128,32},{160,0},{192,96},{224,... | collective-permute-start | bytes 393224 | tf_op jit(solution)/shard_map/ppermute | solution.py:50
  348.1 4.4 copy-start.3
  348.1 31.0 %collective-permute-start.5 = (f32[32,16,64]{2,1,0:T(8,128)S(1)}, f32[32,16,64]{2,1,0:T(8,128)}, u32[]{:S(2)}, u32[]{:S(2)}) collective-permute-start(f32[32,16,64]{2,1,0:T(8,128)S(1)} %get-tuple-element.12), channel_id=1, source_target_pairs={{0,192},{32,224},{64,128},{96,160},{128,64},{160,96},{192,0},{224,... | collective-permute-start | bytes 393224 | tf_op jit(solution)/shard_map/ppermute | solution.py:50
  352.1 0.7 copy-start.2
  352.1 29.3 %collective-permute-start.6 = (f32[32,16,64]{2,1,0:T(8,128)S(1)}, f32[32,16,64]{2,1,0:T(8,128)}, u32[]{:S(2)}, u32[]{:S(2)}) collective-permute-start(f32[32,16,64]{2,1,0:T(8,128)S(1)} %get-tuple-element.11), channel_id=1, source_target_pairs={{0,224},{32,192},{64,160},{96,128},{128,96},{160,64},{192,32},{224... | collective-permute-start | bytes 393224 | tf_op jit(solution)/shard_map/ppermute | solution.py:50
Sparse Core Ops, SparseCore 0:
  25.2 253.2 all-reduce.3
  389.0 249.1 all-reduce.5
